TPU v7x, 32 devices: a whole 2x2x4 slice. The times are simulated.
32 devices in a mesh: group: 2 (over x), hst: 16 (over z, y, core).
Axes of the slice: x: 2, y: 2, z: 4, core: 2. Of those that a mesh axis runs over, the one named last changes fastest.
Arguments:
- tokens: bfloat16 [1024, 4096], P(('group', 'hst')), parts along dimension 0, may hold values from -6 to 6
- routes: int32 [1024, 8], P(('group', 'hst')), parts along dimension 0, may hold values from 0 to 15, all different within a row; in each aligned block of 32 rows (0 to 31, 32 to 63, ...) at most 32 rows name the same one
- gate_code: int32 [1024, 8], P(('group', 'hst')), parts along dimension 0, may hold values from 1 to 65535
- w_gate: bfloat16 [16, 4096, 768], P('hst'), may hold values from -0.09375 to 0.09375
- w_up: bfloat16 [16, 4096, 768], P('hst'), may hold values from -0.09375 to 0.09375
- w_down: bfloat16 [16, 768, 4096], P('hst'), may hold values from -0.21875 to 0.21875
Outputs:
- moe_out: bfloat16 [1024, 4096], P(('group', 'hst')), parts along dimension 0
There are 2 independent parts, one for each index of `group`. A program takes and returns all parts, laid end to end along the dimension named above; an argument that names none is the same for every part. Nothing has to cross between parts.
Inputs may be any that keep to these rules, and one draw needn't show every extreme that they name: `routes`: each row names 8 different experts. Among the rows of one index of hst no expert is named more than 32 times, a bound that some block reaches there in every draw; every expert is named somewhere.
All inputs are finite; a program needn't handle non-finite values.
Results may differ from a plain program's by a relative error of at most 0.008.
Values may be sent and summed in bfloat16 or wider, within the bound.
A program may use at most 128 MiB of HBM per device.

v0:
```python
import jax
import jax.numpy as jnp
from jax import lax
from jax.sharding import PartitionSpec as P


def local(tokens, routes, gate_code, w_gate, w_up, w_down):
    n = lax.axis_size("hst")
    experts = n * w_gate.shape[0]
    me = lax.axis_index("hst")
    codes = gate_code.astype(jnp.float32)
    hits = (routes[:, :, None] == jnp.arange(experts, dtype=jnp.int32)[None, None, :]).astype(jnp.float32)
    weights = jnp.sum(hits * codes[:, :, None], axis=1) / jnp.sum(codes, axis=1, keepdims=True)
    all_weights = lax.all_gather(weights, "hst", axis=0, tiled=True)
    mine = lax.dynamic_slice_in_dim(all_weights, me, 1, axis=1)
    rows = lax.all_gather(tokens, "hst", axis=0, tiled=True)
    gate_h = jnp.dot(rows, w_gate[0], preferred_element_type=jnp.float32)
    up_h = jnp.dot(rows, w_up[0], preferred_element_type=jnp.float32)
    hidden = (jax.nn.silu(gate_h) * up_h).astype(jnp.bfloat16)
    out = jnp.dot(hidden, w_down[0], preferred_element_type=jnp.float32)
    part = (out * mine).astype(jnp.bfloat16)
    return lax.psum_scatter(part, "hst", scatter_dimension=0, tiled=True)


def solution(mesh):
    rows = P(("group", "hst"), None)
    whole = P("hst", None, None)
    return jax.shard_map(local, mesh=mesh, in_specs=(rows, rows, rows, whole, whole, whole), out_specs=rows, check_vma=False)
```

profile of v0, /device:TPU:0, one launch (start us, length us, event | category | flops | bytes accessed | tf_op | source)
XLA Modules:
  0.0 165.0 jit_solution(2642381142673461545)
XLA Ops:
  6.5 0.0 all-gather.3.cloned.1.call-start
  6.5 0.7 all-gather.3.cloned.1.call-update
  7.3 0.0 reduce-scatter.2.cloned.1.call-start
  7.3 0.7 convert_element_type.11
  8.0 0.7 convert_reduce_fusion
  8.7 0.7 select_reduce_fusion
  9.4 23.7 %all-gather = f32[16,32,16]{1,2,0:T(8,128)S(1)} all-gather(f32[1,32,16]{1,2,0:T(8,128)S(1)} %divide_bitcast_fusion), channel_id=1, replica_groups=mesh['group'=2,'hst'=16] {'hst'}, dimensions={0}, use_global_device_ids=true | all-gather | bytes 34816 | tf_op jit(solution)/shard_map/all_gather | solution.py:14
  33.2 0.1 reshape.4
  33.3 29.9 %all-gather.3.cloned.1.call-done = bf16[512,4096]{1,0:T(8,128)(2,1)} async-done(((bf16[32,4096]{1,0:T(8,128)(2,1)}), bf16[512,4096]{1,0:T(8,128)(2,1)}) %all-gather.3.cloned.1.call-update) | async-done | bytes 4194320 | tf_op jit(solution)/shard_map/all_gather | solution.py:16
  63.2 7.0 %fusion.3 = f32[512,768]{1,0:T(8,128)S(1)} fusion(bf16[512,4096]{1,0:T(8,128)(2,1)} %all-gather.3.cloned.1.call-done, bf16[1,4096,768]{2,1,0:T(8,128)(2,1)} %param.9), kind=kOutput, calls=%fused_computation.4 | convolution fusion | flops 3221225472 | bytes 12058624 | tf_op jit(solution)/shard_map/dot_general | solution.py:17
  70.2 16.6 %multiply_convert_fusion = bf16[512,4096]{1,0:T(8,128)(2,1)} fusion(bf16[1,768,4096]{2,1,0:T(8,128)(2,1)} %param.11, f32[512]{0:T(512)S(1)} %bitcast.20, f32[512,768]{1,0:T(8,128)S(1)} %fusion.3, bf16[512,4096]{1,0:T(8,128)(2,1)} %all-gather.3.cloned.1.call-done, bf16[1,4096,768]{2,1,0:T(8,128)(2,1)} %param.10), kind=kOutput, calls=%fused_computation | convolution fusion | flops 6449004544 | bytes 22546432 | tf_op jit(solution)/shard_map/dot_general | solution.py:20
  86.8 0.0 reduce-scatter.2.cloned.1.call-update
  86.9 71.3 %reduce-scatter.2.cloned.1.call-done = bf16[32,4096]{1,0:T(8,128)(2,1)} async-done(((bf16[512,4096]{1,0:T(8,128)(2,1)}), bf16[32,4096]{1,0:T(8,128)(2,1)}) %reduce-scatter.2.cloned.1.call-update) | async-done | bytes 262160 | tf_op jit(solution)/shard_map/reduce_scatter | solution.py:22
  (3 shorter events, 0.1 us)
Async XLA Ops:
  6.5 56.7 %all-gather.3.cloned.1.call-start = ((), (), s32[]{:S(2)}) async-start(), calls=%async_computation.1 | async-start | bytes 4456448 | tf_op jit(solution)/shard_map/all_gather | solution.py:16
  7.3 150.9 %reduce-scatter.2.cloned.1.call-start = ((), (), s32[]{:S(2)}) async-start(), calls=%async_computation.2 | async-start | bytes 4456448 | tf_op jit(solution)/shard_map/reduce_scatter | solution.py:22
Sparse Core Ops, SparseCore 0:
  9.5 53.6 all-gather.2
  87.0 71.0 reduce-scatter.1
where the time goes:
time: 165 us
  waiting for transfers between devices  102 us (62%)
  blocking collectives  23.7 us (14%)
  matrix products  23.6 us (14%)
  between operations  13.4 us (8%)
  other arithmetic  2.1 us (1%)
    reduce_scatter x1, waiting for transfers between devices, local(): return lax.psum_scatter(part, 'hst', scatter_dimension=0, tiled=True)  71.3 us
    all_gather x1, waiting for transfers between devices, local(): rows = lax.all_gather(tokens, 'hst', axis=0, tiled=True)  29.9 us
    all_gather x1, blocking collectives, local(): all_weights = lax.all_gather(weights, 'hst', axis=0, tiled=True)  23.7 us
    dot_general x1, matrix products, local(): out = jnp.dot(hidden, w_down[0], preferred_element_type=jnp.float32)  16.6 us
    dot_general x1, matrix products, local(): gate_h = jnp.dot(rows, w_gate[0], preferred_element_type=jnp.float32)  7.03 us
  transfers between devices with their start and end apart: 2, of which 2 were waited for; matrix products, arithmetic and copies ran while one was open for 1% of the time, Pallas kernels for 0%

commit v1 on v0

v1 whole, which is shorter than its diff:
```python
import functools

import jax
import jax.numpy as jnp
from jax import lax
from jax.experimental import pallas as pl
from jax.experimental.pallas import tpu as pltpu
from jax.sharding import PartitionSpec as P

ROWS = 16
PAD = 128


def kernel(plan, tokens, routes, codes, wg_hbm, wu_hbm, wd_hbm, out, X, PT, HID, RC, RY, RUP, RDN, wg, wu, wd,
           ag_recv, ag_send, c_send, c_recv, y_send, y_recv, up_send, up_recv, dn_send, dn_recv, w_sem):
    Z, Y, C, Q, D, ag_parts, rs_parts = plan
    ZY = Z * Y
    me = lax.axis_index("hst")
    c = lax.rem(me, C)
    y = lax.rem(lax.div(me, C), Y)
    z = lax.div(me, C * Y)
    oc = 1 - c
    oy = 1 - y

    def dev(zz, yy, cc):
        return (zz * Y + yy) * C + cc

    def blk(zz, yy):
        return zz * Y + yy

    def at(q, cc, b):
        return pl.ds(pl.multiple_of(((q * C + cc) * ZY + b) * ROWS, ROWS), ROWS)

    def slot(q, b, count):
        return pl.ds(pl.multiple_of((q * count + b) * ROWS, ROWS), ROWS)

    has_up = z < Z - 1
    has_dn = z > 0

    def when(cond, fn):
        if cond is None:
            fn()
        else:
            pl.when(cond)(fn)

    def both(a, b):
        return b if a is None else (a if b is None else jnp.logical_and(a, b))

    pending = []

    def remote(src, dst, ssem, rsem, to):
        return pltpu.make_async_remote_copy(src_ref=src, dst_ref=dst, send_sem=ssem, recv_sem=rsem,
                                            device_id={"hst": to}, device_id_type=pl.DeviceIdType.MESH)

    def send(cond, make):
        when(cond, lambda: make().start())
        pending.append((cond, make))

    loads = [pltpu.make_async_copy(a, b, w_sem.at[i]) for i, (a, b) in
             enumerate(((wg_hbm, wg), (wu_hbm, wu), (wd_hbm, wd)))]
    for load in loads:
        load.start()

    barrier = pltpu.get_barrier_semaphore()

    def greet(to):
        pl.semaphore_signal(barrier, inc=1, device_id={"hst": to}, device_id_type=pl.DeviceIdType.MESH)

    greet(dev(z, y, oc))
    if Y > 1:
        greet(dev(z, oy, c))
    pl.when(has_up)(lambda: greet(dev(z + 1, y, c)))
    pl.when(has_dn)(lambda: greet(dev(z - 1, y, c)))

    lane = lax.broadcasted_iota(jnp.int32, (Q * ROWS, PAD), 1)
    half = PAD // 2
    expert = lax.rem(lane, half)
    total = jnp.zeros((Q * ROWS, 1), jnp.float32)
    weight = jnp.zeros((Q * ROWS, PAD), jnp.float32)
    for k in range(routes.shape[1]):
        code = codes[:, k:k + 1].astype(jnp.float32)
        total = total + code
        weight = weight + jnp.where(expert == routes[:, k:k + 1], code, 0.0)
    weight = weight / total
    high = weight.astype(jnp.bfloat16).astype(jnp.float32)
    packed = jnp.where(lane < half, high, weight - high).astype(jnp.bfloat16)
    for q in range(Q):
        X[at(q, c, blk(z, y)), 0:D] = tokens[q * ROWS:(q + 1) * ROWS, :]
        X[at(q, c, blk(z, y)), D:D + PAD] = packed[q * ROWS:(q + 1) * ROWS, :]
    pl.semaphore_wait(barrier, 1 + (Y - 1) + has_up.astype(jnp.int32) + has_dn.astype(jnp.int32))

    def ag_send_one(q, p, kind, cc, b, to, cond):
        c0, c1, _ = ag_parts[p]

        def make():
            ref = X.at[at(q, cc, b), c0:c1]
            return remote(ref, ref, ag_send.at[q, p, kind, b], ag_recv.at[q, p, cc * ZY + b], to)
        send(cond, make)

    def ag_wait(q, p, cc, b, cond):
        c0, c1, _ = ag_parts[p]

        def fn():
            ref = X.at[at(q, cc, b), c0:c1]
            remote(ref, ref, ag_send.at[q, p, 0, b], ag_recv.at[q, p, cc * ZY + b], dev(z, y, oc)).wait_recv()
        when(cond, fn)

    def go_up(q, p, b, cond=None):
        ag_send_one(q, p, 0, c, b, dev(z + 1, y, c), both(cond, has_up))

    def go_dn(q, p, b, cond=None):
        ag_send_one(q, p, 1, c, b, dev(z - 1, y, c), both(cond, has_dn))

    def go_y(q, p, b, cond=None):
        ag_send_one(q, p, 2, c, b, dev(z, oy, c), cond)

    def go_c(q, p, b, cond=None):
        ag_send_one(q, p, 3, c, b, dev(z, y, oc), cond)

    def ag_start(q):
        for p, (_, _, first) in enumerate(ag_parts):
            own = blk(z, y)
            if Y > 1:
                go_y(q, p, own)
            go_up(q, p, own)
            go_dn(q, p, own)
            go_c(q, p, own)

    def ag_turn(q):
        for p, (_, _, first) in enumerate(ag_parts):
            if first == "y":
                b = blk(z, oy)
                ag_wait(q, p, c, b, None)
                go_up(q, p, b)
                go_dn(q, p, b)
                go_c(q, p, b)

    def ag_step(q, s):
        for p, (_, _, first) in enumerate(ag_parts):
            for yy in ((y, oy) if first == "y" else (y,)):
                lo, hi = z - s, z + s
                ok_lo, ok_hi = lo >= 0, hi < Z
                ag_wait(q, p, c, blk(lo, yy), ok_lo)
                go_up(q, p, blk(lo, yy), ok_lo)
                if first == "z" and Y > 1:
                    go_y(q, p, blk(lo, yy), ok_lo)
                ag_wait(q, p, c, blk(hi, yy), ok_hi)
                go_dn(q, p, blk(hi, yy), ok_hi)
                if first == "z" and Y > 1:
                    go_y(q, p, blk(hi, yy), ok_hi)
                go_c(q, p, blk(lo, yy), ok_lo)
                go_c(q, p, blk(hi, yy), ok_hi)

    def ag_cross(q, s):
        for p, (_, _, first) in enumerate(ag_parts):
            if first == "z" and Y > 1:
                if s == 0:
                    ag_wait(q, p, c, blk(z, oy), None)
                    go_c(q, p, blk(z, oy))
                else:
                    for far, ok in ((z - s, z - s >= 0), (z + s, z + s < Z)):
                        ag_wait(q, p, c, blk(far, oy), ok)
                        go_c(q, p, blk(far, oy), ok)

    def ag_end(q):
        for p in range(len(ag_parts)):
            for b in range(ZY):
                ag_wait(q, p, oc, b, None)

    rows_all = C * ZY * ROWS
    F = wg.shape[1]
    tile_f = 256 if F % 256 == 0 else F
    tile_d = 512

    def gate_up(q, j):
        cols = slice(j * tile_f, (j + 1) * tile_f)
        rows = X[q * rows_all:(q + 1) * rows_all, 0:D]
        g = jnp.dot(rows, wg[:, cols], preferred_element_type=jnp.float32)
        u = jnp.dot(rows, wu[:, cols], preferred_element_type=jnp.float32)
        HID[:, cols] = (g / (1.0 + jnp.exp(-g)) * u).astype(jnp.bfloat16)

    def down(q, d0, d1):
        lanes = lax.broadcasted_iota(jnp.int32, (rows_all, PAD), 1)
        both_parts = X[q * rows_all:(q + 1) * rows_all, D:D + PAD].astype(jnp.float32)
        col = jnp.sum(jnp.where(lax.rem(lanes, half) == me, both_parts, 0.0), axis=1, keepdims=True)

        def body(i, carry):
            cols = pl.ds(pl.multiple_of(i * tile_d, tile_d), tile_d)
            o = jnp.dot(HID[...], wd[:, cols], preferred_element_type=jnp.float32)
            PT[q * rows_all:(q + 1) * rows_all, cols] = (o * col).astype(jnp.bfloat16)
            return carry
        lax.fori_loop(d0 // tile_d, d1 // tile_d, body, 0)

    def c_copy(q, p):
        c0, c1, _ = rs_parts[p]
        src = PT.at[pl.ds(pl.multiple_of((q * C + oc) * ZY * ROWS, ROWS), ZY * ROWS), c0:c1]
        dst = RC.at[q * ZY * ROWS:(q + 1) * ZY * ROWS, c0:c1]
        return remote(src, dst, c_send.at[q, p], c_recv.at[q, p], dev(z, y, oc))

    def y_copy(q, p, b, zz):
        c0, c1, _ = rs_parts[p]
        return remote(PT.at[at(q, c, b), c0:c1], RY.at[slot(q, zz, Z), c0:c1],
                      y_send.at[q, p, zz], y_recv.at[q, p, zz], dev(z, oy, c))

    def up_copy(q, p, b):
        c0, c1, _ = rs_parts[p]
        return remote(PT.at[at(q, c, b), c0:c1], RUP.at[slot(q, b, ZY), c0:c1],
                      up_send.at[q, p, b], up_recv.at[q, p, b], dev(z + 1, y, c))

    def dn_copy(q, p, b):
        c0, c1, _ = rs_parts[p]
        return remote(PT.at[at(q, c, b), c0:c1], RDN.at[slot(q, b, ZY), c0:c1],
                      dn_send.at[q, p, b], dn_recv.at[q, p, b], dev(z - 1, y, c))

    def add(p, dst, dst_rows, terms):
        c0, c1, _ = rs_parts[p]
        tile = 512 if (c1 - c0) % 512 == 0 and c0 % 512 == 0 else 128

        def body(i, carry):
            cols = pl.ds(pl.multiple_of(i * tile, tile), tile)
            s = terms[0][0][terms[0][1], cols].astype(jnp.float32)
            for ref, r in terms[1:]:
                s = s + ref[r, cols].astype(jnp.float32)
            dst[dst_rows, cols] = s.astype(jnp.bfloat16)
            return carry
        lax.fori_loop(c0 // tile, c1 // tile, body, 0)

    def rs_start(q):
        for p in range(len(rs_parts)):
            send(None, lambda p=p: c_copy(q, p))

    def rs_sibling(q):
        for p, (_, _, last) in enumerate(rs_parts):
            c_copy(q, p).wait_recv()

    def rs_cross(q, s):
        for p, (_, _, last) in enumerate(rs_parts):
            if last == "z" and Y > 1:
                for zz, ok in (((z - s, z - s >= 0), (z + s, z + s < Z)) if s else ((z, None),)):
                    b = blk(zz, oy)
                    when(ok, lambda b=b, p=p: add(p, PT, at(q, c, b), [(PT, at(q, c, b)), (RC, slot(q, b, ZY))]))
                    send(ok, lambda b=b, p=p, zz=zz: y_copy(q, p, b, zz))

    def base_terms(q, p, b, zz):
        terms = [(PT, at(q, c, b)), (RC, slot(q, b, ZY))]
        if rs_parts[p][2] == "z" and Y > 1:
            y_copy(q, p, b, zz).wait_recv()
            terms.append((RY, slot(q, zz, Z)))
        return terms

    def rs_step(q, s):
        for p, (_, _, last) in enumerate(rs_parts):
            for yy in ((oy, y) if last == "y" else (y,)):
                for far, ok, more, copy, R in ((z - s, z - s >= 0, has_up, dn_copy, RDN),
                                               (z + s, z + s < Z, has_dn, up_copy, RUP)):
                    b = blk(far, yy)

                    def fn(b=b, p=p, far=far, more=more, copy=copy, R=R):
                        terms = base_terms(q, p, b, far)

                        @pl.when(more)
                        def _():
                            copy(q, p, b).wait_recv()
                            add(p, PT, at(q, c, b), terms + [(R, slot(q, b, ZY))])

                        @pl.when(jnp.logical_not(more))
                        def _():
                            add(p, PT, at(q, c, b), terms)
                    when(ok, fn)
                    send(ok, lambda b=b, p=p, copy=copy: copy(q, p, b))

    def rs_final(q):
        for p, (_, _, last) in enumerate(rs_parts):
            for yy in ((oy, y) if last == "y" else (y,)):
                b = blk(z, yy)
                terms = base_terms(q, p, b, z)
                pl.when(has_up)(lambda p=p, b=b: dn_copy(q, p, b).wait_recv())
                pl.when(has_dn)(lambda p=p, b=b: up_copy(q, p, b).wait_recv())
                up_term, dn_term = (RUP, slot(q, b, ZY)), (RDN, slot(q, b, ZY))
                if last == "y":
                    dst, dst_rows = PT, at(q, c, b)
                else:
                    dst, dst_rows = out, slice(q * ROWS, (q + 1) * ROWS)
                pl.when(jnp.logical_and(has_up, has_dn))(
                    lambda p=p, t=terms, u=up_term, d=dn_term, a=dst, r=dst_rows: add(p, a, r, t + [u, d]))
                pl.when(jnp.logical_not(has_up))(
                    lambda p=p, t=terms, u=up_term, a=dst, r=dst_rows: add(p, a, r, t + [u]))
                pl.when(jnp.logical_not(has_dn))(
                    lambda p=p, t=terms, d=dn_term, a=dst, r=dst_rows: add(p, a, r, t + [d]))
                if last == "y" and yy is oy:
                    send(None, lambda p=p, b=b: y_copy(q, p, b, z))

    def rs_last(q):
        for p, (_, _, last) in enumerate(rs_parts):
            if last == "y":
                b = blk(z, y)
                y_copy(q, p, b, z).wait_recv()
                add(p, out, slice(q * ROWS, (q + 1) * ROWS), [(PT, at(q, c, b)), (RY, slot(q, z, Z))])

    def ag_list(q):
        return ([lambda: ag_start(q), lambda: ag_turn(q)]
                + [lambda s=s: ag_step(q, s) for s in range(1, Z)]
                + [lambda s=s: ag_cross(q, s) for s in range(Z)] + [lambda: ag_end(q)])

    def ffn_list(q):
        def first(j):
            if q == 0 and j == 0:
                loads[0].wait()
                loads[1].wait()
            gate_up(q, j)

        def last(d0, d1):
            if q == 0 and d0 == 0:
                loads[2].wait()
            down(q, d0, d1)
        return [lambda j=j: first(j) for j in range(F // tile_f)] + [lambda: last(0, D)]

    def rs_list(q):
        return ([lambda: rs_start(q), lambda: rs_sibling(q)]
                + [lambda s=s: rs_cross(q, s) for s in range(Z - 1, -1, -1)]
                + [lambda s=s: rs_step(q, s) for s in range(Z - 1, 0, -1)]
                + [lambda: rs_final(q), lambda: rs_last(q)])

    def run(*lists):
        longest = max(len(a) for a in lists)
        places = []
        for n, a in enumerate(lists):
            places += [((i + 1) / (len(a) + 1), n, f) for i, f in enumerate(a)]
        for _, _, f in sorted(places, key=lambda t: t[:2]):
            f()
        del longest

    run(ag_list(0))
    for q in range(Q):
        if q + 1 < Q:
            run(ag_list(q + 1), ffn_list(q)) if q == 0 else run(ag_list(q + 1), ffn_list(q), rs_list(q - 1))
        elif q:
            run(ffn_list(q), rs_list(q - 1))
        else:
            run(ffn_list(q))
    run(rs_list(Q - 1))
    for cond, make in pending:
        when(cond, lambda make=make: make().wait_send())


def local(shape, tokens, routes, gate_code, w_gate, w_up, w_down):
    Z, Y, C, ag_cut, rs_cut = shape
    n = Z * Y * C
    rows, D = tokens.shape
    F = w_gate.shape[2]
    Q = rows // ROWS
    wide = D + PAD
    ag_parts = tuple((a, b, m) for a, b, m in ((0, ag_cut, "y"), (ag_cut, wide, "z")) if b > a)
    rs_parts = tuple((a, b, m) for a, b, m in ((0, rs_cut, "y"), (rs_cut, D, "z")) if b > a)
    NA, NR, ZY = len(ag_parts), len(rs_parts), Z * Y
    plan = (Z, Y, C, Q, D, ag_parts, rs_parts)
    bf = jnp.bfloat16
    dma = pltpu.SemaphoreType.DMA
    vmem = pl.BlockSpec(memory_space=pltpu.VMEM)
    hbm = pl.BlockSpec(memory_space=pl.ANY)
    z_rows = Q * ZY * ROWS
    return pl.pallas_call(
        functools.partial(kernel, plan),
        out_shape=jax.ShapeDtypeStruct((rows, D), bf),
        in_specs=[vmem, vmem, vmem, hbm, hbm, hbm],
        out_specs=vmem,
        scratch_shapes=[
            pltpu.VMEM((Q * n * ROWS, wide), bf),
            pltpu.VMEM((Q * n * ROWS, D), bf),
            pltpu.VMEM((n * ROWS, F), bf),
            pltpu.VMEM((z_rows, D), bf),
            pltpu.VMEM((Q * Z * ROWS, D), bf),
            pltpu.VMEM((z_rows, D), bf),
            pltpu.VMEM((z_rows, D), bf),
            pltpu.VMEM((D, F), bf),
            pltpu.VMEM((D, F), bf),
            pltpu.VMEM((F, D), bf),
            dma((Q, NA, n)), dma((Q, NA, 4, ZY)),
            dma((Q, NR)), dma((Q, NR)),
            dma((Q, NR, Z)), dma((Q, NR, Z)),
            dma((Q, NR, ZY)), dma((Q, NR, ZY)),
            dma((Q, NR, ZY)), dma((Q, NR, ZY)),
            dma((3,)),
        ],
        compiler_params=pltpu.CompilerParams(
            collective_id=0, has_side_effects=True, vmem_limit_bytes=60 * 1024 * 1024),
    )(tokens, routes, gate_code, w_gate[0], w_up[0], w_down[0])


def solution(mesh):
    n = mesh.shape["hst"]
    C = 2
    Y = 2 if n <= 16 else 1
    shape = (n // (C * Y), Y, C, AG_CUT if Y > 1 else 0, RS_CUT if Y > 1 else 0)
    rows = P(("group", "hst"), None)
    whole = P("hst", None, None)
    return jax.shard_map(functools.partial(local, shape), mesh=mesh,
                         in_specs=(rows, rows, rows, whole, whole, whole), out_specs=rows, check_vma=False)


AG_CUT = 1536
RS_CUT = 1536
```

time: 165 us -> 89.1 us (0.54)
  the two profiles are of different devices: /device:TPU:0 before, /device:TPU:1 now
where the time goes in v1:
time: 89.1 us; the launch traced here: 88.8 us
  Pallas kernels  84.4 us (95%)
  local copies, waits for them, and re-layouts  4.39 us (5%)
    pallas_call x1, Pallas kernels, local(): pl.pallas_call(functools.partial(kernel, plan), out_shape=jax.ShapeDtypeS...  84.4 us
    unnamed x3, local copies, waits for them, and re-layouts  4.39 us

profile of v1, /device:TPU:1, one launch (start us, length us, event | category | flops | bytes accessed | tf_op | source)
XLA Modules:
  0.0 88.8 jit_solution(11857908286781114372)
XLA Ops:
  0.0 1.4 %copy.7.routes = s32[32,8]{1,0:T(8,128)} copy(s32[32,8]{0,1:T(8,128)} %param.7) | data formatting | bytes 2048 | tf_op args[1]
  1.4 1.4 %copy.8.codes = s32[32,8]{1,0:T(8,128)} copy(s32[32,8]{0,1:T(8,128)} %param.8) | data formatting | bytes 2048 | tf_op args[2]
  2.7 84.4 %shard_map.64 = bf16[32,4096]{1,0:T(8,128)(2,1)} custom-call(bf16[32,4096]{1,0:T(8,128)(2,1)} %tokens.1, s32[32,8]{1,0:T(8,128)} %copy.7.routes, s32[32,8]{1,0:T(8,128)} %copy.8.codes, bf16[4096,768]{1,0:T(8,128)(2,1)} %bitcast.3, bf16[4096,768]{1,0:T(8,128)(2,1)} %bitcast.4, bf16[768,4096]{1,0:T(8,128)(2,1)} %bitcast.5), custom_call_target="tpu_custom_call" | custom-call | tf_op jit(solution)/shard_map/pallas_call | solution.py:362
  87.2 1.7 %copy.10 = bf16[32,4096]{1,0:T(8,128)(2,1)} copy(bf16[32,4096]{1,0:T(8,128)(2,1)} %shard_map.64) | data formatting | bytes 524288

commit v2 on v1

--- a/solution.py
+++ b/solution.py
@@ -72,18 +72,22 @@
     pl.when(has_up)(lambda: greet(dev(z + 1, y, c)))
     pl.when(has_dn)(lambda: greet(dev(z - 1, y, c)))
 
-    lane = lax.broadcasted_iota(jnp.int32, (Q * ROWS, PAD), 1)
     half = PAD // 2
-    expert = lax.rem(lane, half)
-    total = jnp.zeros((Q * ROWS, 1), jnp.float32)
-    weight = jnp.zeros((Q * ROWS, PAD), jnp.float32)
-    for k in range(routes.shape[1]):
-        code = codes[:, k:k + 1].astype(jnp.float32)
+    spot = lax.broadcasted_iota(jnp.int32, (PAD, Q * ROWS), 0)
+    expert = lax.rem(spot, half)
+    total = jnp.zeros((1, Q * ROWS), jnp.float32)
+    weight = jnp.zeros((PAD, Q * ROWS), jnp.float32)
+    for k in range(routes.shape[0]):
+        code = codes[k:k + 1, :].astype(jnp.float32)
         total = total + code
-        weight = weight + jnp.where(expert == routes[:, k:k + 1], code, 0.0)
+        weight = weight + jnp.where(expert == routes[k:k + 1, :], code, 0.0)
     weight = weight / total
     high = weight.astype(jnp.bfloat16).astype(jnp.float32)
-    packed = jnp.where(lane < half, high, weight - high).astype(jnp.bfloat16)
+    columns = jnp.where(spot < half, high, weight - high).astype(jnp.bfloat16)
+    same = (lax.broadcasted_iota(jnp.int32, (Q * ROWS, Q * ROWS), 0)
+            == lax.broadcasted_iota(jnp.int32, (Q * ROWS, Q * ROWS), 1)).astype(jnp.float32).astype(jnp.bfloat16)
+    packed = lax.dot_general(same, columns, (((1,), (1,)), ((), ())),
+                             preferred_element_type=jnp.float32).astype(jnp.bfloat16)
     for q in range(Q):
         X[at(q, c, blk(z, y)), 0:D] = tokens[q * ROWS:(q + 1) * ROWS, :]
         X[at(q, c, blk(z, y)), D:D + PAD] = packed[q * ROWS:(q + 1) * ROWS, :]
@@ -248,8 +252,10 @@
             terms.append((RY, slot(q, zz, Z)))
         return terms
 
-    def rs_step(q, s):
+    def rs_step(q, s, only):
         for p, (_, _, last) in enumerate(rs_parts):
+            if p != only:
+                continue
             for yy in ((oy, y) if last == "y" else (y,)):
                 for far, ok, more, copy, R in ((z - s, z - s >= 0, has_up, dn_copy, RDN),
                                                (z + s, z + s < Z, has_dn, up_copy, RUP)):
@@ -298,9 +304,10 @@
                 add(p, out, slice(q * ROWS, (q + 1) * ROWS), [(PT, at(q, c, b)), (RY, slot(q, z, Z))])
 
     def ag_list(q):
-        return ([lambda: ag_start(q), lambda: ag_turn(q)]
-                + [lambda s=s: ag_step(q, s) for s in range(1, Z)]
-                + [lambda s=s: ag_cross(q, s) for s in range(Z)] + [lambda: ag_end(q)])
+        events = [lambda: ag_start(q), lambda: ag_turn(q)]
+        for s in range(1, Z):
+            events += [lambda s=s: ag_step(q, s), lambda s=s: ag_cross(q, s - 1)]
+        return events + [lambda: ag_cross(q, Z - 1), lambda: ag_end(q)]
 
     def ffn_list(q):
         def first(j):
@@ -313,32 +320,52 @@
             if q == 0 and d0 == 0:
                 loads[2].wait()
             down(q, d0, d1)
-        return [lambda j=j: first(j) for j in range(F // tile_f)] + [lambda: last(0, D)]
+        return [lambda j=j: first(j) for j in range(F // tile_f)] + [lambda: last(0, D // 2), lambda: last(D // 2, D)]
 
     def rs_list(q):
-        return ([lambda: rs_start(q), lambda: rs_sibling(q)]
-                + [lambda s=s: rs_cross(q, s) for s in range(Z - 1, -1, -1)]
-                + [lambda s=s: rs_step(q, s) for s in range(Z - 1, 0, -1)]
-                + [lambda: rs_final(q), lambda: rs_last(q)])
+        parts = range(len(rs_parts))
+        events = [lambda: rs_sibling(q)]
+        for s in range(Z - 1, -1, -1):
+            events.append(lambda s=s: rs_cross(q, s))
+        for n, s in enumerate(range(Z - 1, 0, -1)):
+            for p in parts:
+                place = 2 + n + 2 * (n + 1) if rs_parts[p][2] == "z" else 2 + 2 * n + n
+                events.insert(min(place, len(events)), lambda s=s, p=p: rs_step(q, s, p))
+        return events + [lambda: rs_final(q), lambda: rs_last(q)]
 
     def run(*lists):
-        longest = max(len(a) for a in lists)
         places = []
         for n, a in enumerate(lists):
             places += [((i + 1) / (len(a) + 1), n, f) for i, f in enumerate(a)]
-        for _, _, f in sorted(places, key=lambda t: t[:2]):
+        for _, _, f in sorted(places, key=lambda e: e[:2]):
             f()
-        del longest
-
-    run(ag_list(0))
+
+    def lagged(a, b, lag):
+        for i in range(max(len(a), len(b) + lag)):
+            if i < len(a):
+                a[i]()
+            if 0 <= i - lag < len(b):
+                b[i - lag]()
+
+    ahead = ag_list(0)
+    later = ag_list(1) if Q > 1 else []
+    lagged(ahead, later[:len(ahead) - AG_LAG], AG_LAG)
+    later = later[len(ahead) - AG_LAG:]
+    before = []
     for q in range(Q):
-        if q + 1 < Q:
-            run(ag_list(q + 1), ffn_list(q)) if q == 0 else run(ag_list(q + 1), ffn_list(q), rs_list(q - 1))
-        elif q:
-            run(ffn_list(q), rs_list(q - 1))
+        k = min(RS_EARLY, len(before))
+        run(ffn_list(q), later if q == 0 else before[:k])
+        rs_start(q)
+        if q == 0:
+            before = rs_list(0)
         else:
-            run(ffn_list(q))
-    run(rs_list(Q - 1))
+            if q + 1 < Q:
+                run(ag_list(q + 1), before[k:])
+                before = rs_list(q)
+            else:
+                lagged(before[k:], rs_list(q), RS_LAG)
+                before = []
+    run(before)
     for cond, make in pending:
         when(cond, lambda make=make: make().wait_send())
 
@@ -384,7 +411,7 @@
         ],
         compiler_params=pltpu.CompilerParams(
             collective_id=0, has_side_effects=True, vmem_limit_bytes=60 * 1024 * 1024),
-    )(tokens, routes, gate_code, w_gate[0], w_up[0], w_down[0])
+    )(tokens, routes.T, gate_code.T, w_gate[0], w_up[0], w_down[0])
 
 
 def solution(mesh):
@@ -398,5 +425,8 @@
                          in_specs=(rows, rows, rows, whole, whole, whole), out_specs=rows, check_vma=False)
 
 
-AG_CUT = 1536
-RS_CUT = 1536
+AG_CUT = 0
+RS_CUT = 512
+AG_LAG = 3
+RS_EARLY = 5
+RS_LAG = 1

time: 89.1 us -> 72.1 us (0.81)
  the two profiles are of different devices: /device:TPU:1 before, /device:TPU:0 now
where the time goes in v2:
time: 72.1 us; the launch traced here: 72 us
  Pallas kernels  70.3 us (98%)
  local copies, waits for them, and re-layouts  1.67 us (2%)
    pallas_call x1, Pallas kernels, local(): pl.pallas_call(functools.partial(kernel, plan), out_shape=jax.ShapeDtypeS...  70.3 us
    unnamed x1, local copies, waits for them, and re-layouts  1.67 us

profile of v2, /device:TPU:0, one launch (start us, length us, event | category | flops | bytes accessed | tf_op | source)
XLA Modules:
  0.0 72.0 jit_solution(11894153062440586529)
XLA Ops:
  0.0 70.3 %shard_map.64 = bf16[32,4096]{1,0:T(8,128)(2,1)} custom-call(bf16[32,4096]{1,0:T(8,128)(2,1)} %tokens.1, s32[8,32]{1,0:T(8,128)} %bitcast.8, s32[8,32]{1,0:T(8,128)} %bitcast.9, bf16[4096,768]{1,0:T(8,128)(2,1)} %bitcast.5, bf16[4096,768]{1,0:T(8,128)(2,1)} %bitcast.6, bf16[768,4096]{1,0:T(8,128)(2,1)} %bitcast.7), custom_call_target="tpu_custom_call" | custom-call | tf_op jit(solution)/shard_map/pallas_call | solution.py:389
  70.3 1.7 %copy.8 = bf16[32,4096]{1,0:T(8,128)(2,1)} copy(bf16[32,4096]{1,0:T(8,128)(2,1)} %shard_map.64) | data formatting | bytes 524288

commit v3 on v2

--- a/solution.py
+++ b/solution.py
@@ -377,7 +377,7 @@
     F = w_gate.shape[2]
     Q = rows // ROWS
     wide = D + PAD
-    ag_parts = tuple((a, b, m) for a, b, m in ((0, ag_cut, "y"), (ag_cut, wide, "z")) if b > a)
+    ag_parts = tuple((a, b, m) for a, b, m in ((0, ag_cut, "y"), (ag_cut, D // 2, "z"), (D // 2, wide, "z")) if b > a)
     rs_parts = tuple((a, b, m) for a, b, m in ((0, rs_cut, "y"), (rs_cut, D, "z")) if b > a)
     NA, NR, ZY = len(ag_parts), len(rs_parts), Z * Y
     plan = (Z, Y, C, Q, D, ag_parts, rs_parts)

time: 72.1 us -> 71.8 us (level)
  no operation moved by 1% of the time
where the time goes in v3:
time: 71.8 us; the launch traced here: 71.4 us
  Pallas kernels  69.7 us (97%)
  local copies, waits for them, and re-layouts  1.67 us (2%)
    pallas_call x1, Pallas kernels, local(): pl.pallas_call(functools.partial(kernel, plan), out_shape=jax.ShapeDtypeS...  69.7 us
    unnamed x1, local copies, waits for them, and re-layouts  1.67 us

profile of v3, /device:TPU:0, one launch (start us, length us, event | category | flops | bytes accessed | tf_op | source)
XLA Modules:
  0.0 71.4 jit_solution(4503049579654537029)
XLA Ops:
  0.0 69.7 %shard_map.64 = bf16[32,4096]{1,0:T(8,128)(2,1)} custom-call(bf16[32,4096]{1,0:T(8,128)(2,1)} %tokens.1, s32[8,32]{1,0:T(8,128)} %bitcast.8, s32[8,32]{1,0:T(8,128)} %bitcast.9, bf16[4096,768]{1,0:T(8,128)(2,1)} %bitcast.5, bf16[4096,768]{1,0:T(8,128)(2,1)} %bitcast.6, bf16[768,4096]{1,0:T(8,128)(2,1)} %bitcast.7), custom_call_target="tpu_custom_call" | custom-call | tf_op jit(solution)/shard_map/pallas_call | solution.py:389
  69.7 1.7 %copy.8 = bf16[32,4096]{1,0:T(8,128)(2,1)} copy(bf16[32,4096]{1,0:T(8,128)(2,1)} %shard_map.64) | data formatting | bytes 524288
